TPU v7x, 32 devices: a whole 2x2x4 slice. The times are simulated.
32 devices in a mesh: groups: 2 (over y), fsdp: 8 (over z, core), band: 2 (over x).
Axes of the slice: x: 2, y: 2, z: 4, core: 2. Of those that a mesh axis runs over, the one named last changes fastest.
Arguments:
- hidden_in: bfloat16 [16, 4, 64, 5632], P(('groups', 'fsdp'), 'band'), parts along dimension 0, may hold values from -6 to 6
- tap_weights: bfloat16 [9, 5632], P(None, 'fsdp'), may hold values from -2 to 2
- tap_bias: bfloat16 [5632], P('fsdp'), may hold values from -3 to 3
- w_out: bfloat16 [2816, 2240], P('fsdp'), may hold values from -0.109375 to 0.109375
- cotangent: bfloat16 [16, 4, 64, 2240], P(('groups', 'fsdp'), 'band'), parts along dimension 0, may hold values from -0.59765625 to 0.59765625
Outputs:
- block_out: bfloat16 [16, 4, 64, 2240], P(('groups', 'fsdp'), 'band'), parts along dimension 0
- d_hidden: bfloat16 [16, 4, 64, 5632], P(('groups', 'fsdp'), 'band'), parts along dimension 0
- d_taps: float32 [18, 5632], P('groups', 'fsdp'), parts along dimension 0
- d_tap_bias: float32 [11264], P(('groups', 'fsdp')), parts along dimension 0
There are 2 independent parts, one for each index of `groups`. A program takes and returns all parts, laid end to end along the dimension named above; an argument that names none is the same for every part. Nothing has to cross between parts.
All inputs are finite; a program needn't handle non-finite values.
Results may differ from a plain program's by a relative error of at most 0.0049.
Values may be sent and summed in bfloat16 or wider, within the bound.
A program may use at most 128 MiB of HBM per device.

v0:
```python
import jax
import jax.numpy as jnp
from jax import lax
from jax.sharding import PartitionSpec as P


def with_halo(cells, sides, width):
    for axis, dim in sides:
        count = lax.axis_size(axis)
        ends = count - 1
        head = lax.slice_in_dim(cells, 0, width, axis=dim)
        tail = lax.slice_in_dim(cells, cells.shape[dim] - width, cells.shape[dim], axis=dim)
        cells = jnp.concatenate(
            [
                lax.ppermute(tail, axis, [(i, (i + 1) % count) for i in range(ends)]),
                cells,
                lax.ppermute(head, axis, [((i + 1) % count, i) for i in range(ends)]),
            ],
            axis=dim,
        )
    return cells


def body(hidden_in, tap_weights, tap_bias, w_out, cotangent):
    kernel_all, offset_all = (
        lax.all_gather(tap_weights, "fsdp", axis=1, tiled=True),
        lax.all_gather(tap_bias, "fsdp", axis=0, tiled=True),
    )
    kernel = kernel_all.astype(jnp.float32)
    offset = offset_all.astype(jnp.float32)
    image_count, row_count, col_count, channels = hidden_in.shape
    hidden_units = channels // 2
    token_count = image_count * row_count * col_count
    extended = with_halo(hidden_in, (("band", 1),), 1)
    padded = jnp.pad(extended, ((0, 0), (0, 0), (1, 1), (0, 0)))
    summed = jnp.zeros((image_count, row_count, col_count, channels), jnp.float32) + offset
    for tap_row in range(3):
        for tap_col in range(3):
            window = padded[:, tap_row : tap_row + row_count, tap_col : tap_col + col_count, :]
            summed = summed + kernel[3 * tap_row + tap_col] * window
    values_half = summed[..., :hidden_units]
    gate_half = summed[..., hidden_units:]
    sigmoid_gate = jax.nn.sigmoid(gate_half)
    silu_gate = gate_half * sigmoid_gate
    glu_flat = (values_half * silu_gate).astype(jnp.bfloat16).reshape(token_count, hidden_units)
    grad_flat = cotangent.reshape(token_count, cotangent.shape[3])
    features = grad_flat.shape[1]
    piece = lax.all_gather(w_out, "fsdp", axis=0, tiled=True)
    out_sum = jnp.dot(glu_flat, piece, preferred_element_type=jnp.float32)
    d_piece = lax.dot_general(
        grad_flat, piece, (((1,), (1,)), ((), ())), preferred_element_type=jnp.float32
    )
    out_sum, d_glu = (out_sum, d_piece)
    block_out = out_sum.astype(jnp.bfloat16).reshape(image_count, row_count, col_count, features)
    d_glu = d_glu.reshape(image_count, row_count, col_count, hidden_units)
    slope = sigmoid_gate * (1.0 + gate_half * (1.0 - sigmoid_gate))
    d_pre = jnp.concatenate([d_glu * silu_gate, d_glu * values_half * slope], axis=-1).astype(
        jnp.bfloat16
    )
    d_extended = with_halo(d_pre, (("band", 1),), 1)
    d_pad = jnp.pad(d_extended, ((0, 0), (0, 0), (1, 1), (0, 0)))
    d_image = jnp.zeros((image_count, row_count, col_count, channels), jnp.float32)
    tap_terms = []
    for tap_row in range(3):
        for tap_col in range(3):
            d_window = d_pad[
                :, 2 - tap_row : 2 - tap_row + row_count, 2 - tap_col : 2 - tap_col + col_count, :
            ]
            d_image = d_image + kernel[3 * tap_row + tap_col] * d_window
            window = padded[:, tap_row : tap_row + row_count, tap_col : tap_col + col_count, :]
            tap_terms.append(
                jnp.einsum("srck,srck->k", window, d_pre, preferred_element_type=jnp.float32)
            )
    d_hidden = d_image.astype(jnp.bfloat16)
    tap_grad = jnp.stack(tap_terms)
    bias_grad = jnp.sum(d_pre.astype(jnp.float32), axis=(0, 1, 2))
    tap_grad, bias_grad = lax.psum((tap_grad, bias_grad), "band")
    tap_share, bias_share = (
        lax.psum_scatter(tap_grad, "fsdp", scatter_dimension=1, tiled=True),
        lax.psum_scatter(bias_grad, "fsdp", scatter_dimension=0, tiled=True),
    )
    return (block_out, d_hidden, tap_share, bias_share)


def solution(mesh):
    placed = (
        P(("groups", "fsdp"), "band", None, None),
        P(None, "fsdp"),
        P("fsdp"),
        P("fsdp", None),
        P(("groups", "fsdp"), "band", None, None),
    )
    return jax.shard_map(
        body,
        mesh=mesh,
        in_specs=placed,
        out_specs=(
            P(("groups", "fsdp"), "band", None, None),
            P(("groups", "fsdp"), "band", None, None),
            P("groups", "fsdp"),
            P(("groups", "fsdp")),
        ),
        check_vma=False,
    )
```

profile of v0, /device:TPU:0, one launch (start us, length us, event | category | flops | bytes accessed | tf_op | source)
XLA Modules:
  0.0 235.9 jit_solution(369298379283991862)
XLA Ops:
  7.3 0.7 all-gather.3.cloned.1.call-update
  8.0 2.6 %fusion.26 = (bf16[1,1,64,5632]{3,2,1,0:T(8,128)(2,1)}, bf16[1,1,64,5632]{3,2,1,0:T(8,128)(2,1)}) fusion(bf16[1,2,64,5632]{3,2,1,0:T(8,128)(2,1)} %param.5), kind=kLoop, calls=%fused_computation.70 | loop fusion | bytes 2883584 | tf_op jit(solution)/shard_map/slice | solution.py:11
  10.6 1.3 collective-permute-start.1
  11.9 4.9 %collective-permute-start = (bf16[1,1,64,5632]{3,2,1,0:T(8,128)(2,1)}, bf16[1,1,64,5632]{3,2,1,0:T(8,128)(2,1)S(1)}, u32[]{:S(2)}, u32[]{:S(2)}) collective-permute-start(bf16[1,1,64,5632]{3,2,1,0:T(8,128)(2,1)} %get-tuple-element.40), channel_id=1, source_target_pairs={{0,1},{2,3},{4,5},{6,7},{8,9},{10,11},{12,13},{14,15},{16,17},{18,... | collective-permute-start | bytes 2162696 | tf_op jit(solution)/shard_map/ppermute | solution.py:15
  18.3 30.7 %all-reduce.2 = bf16[5632]{0:T(1024)(128)(2,1)S(1)} all-reduce(bf16[5632]{0:T(1024)(128)(2,1)S(1)} %dynamic-update-slice), channel_id=1, replica_groups=mesh['groups'=2,'fsdp'=8,'band'=2] {'fsdp'}, use_global_device_ids=true, to_apply=%add.2 | all-reduce | flops 5632 | bytes 22528
  49.6 25.2 %all-gather = bf16[8,704,9]{1,2,0:T(8,128)(2,1)S(1)} all-gather(bf16[1,704,9]{1,2,0:T(8,128)(2,1)S(1)} %bitcast.101), channel_id=1, replica_groups=mesh['groups'=2,'fsdp'=8,'band'=2] {'fsdp'}, dimensions={0}, use_global_device_ids=true | all-gather | bytes 114048 | tf_op jit(solution)/shard_map/all_gather | solution.py:26
  74.8 0.7 copy_convert_fusion
  75.5 1.8 reshape.190
  78.0 2.4 %slice_reduce_fusion.8 = (f32[5632]{0:T(1024)S(1)}, f32[5632]{0:T(1024)S(1)}, f32[5632]{0:T(1024)S(1)}, f32[5632]{0:T(1024)S(1)}, f32[5632]{0:T(1024)S(1)}, /*in...) fusion(f32[9,5632]{1,0:T(8,128)} %bitcast.97), kind=kLoop, calls=%fused_computation.69 | loop fusion | bytes 405504 | tf_op jit(solution)/shard_map/slice | solution.py:40
  80.5 1.1 select_maximum_fusion.3
  81.7 1.6 copy-done.1
  83.2 3.9 %multiply_add_fusion = f32[1,2,64,5632]{3,2,1,0:T(8,128)} fusion(bf16[1,2,64,5632]{3,2,1,0:T(8,128)(2,1)S(1)} %copy-done.3, f32[5632]{0:T(1024)S(1)} %get-tuple-element.18, f32[5632]{0:T(1024)S(1)} %get-tuple-element.19, f32[5632]{0:T(1024)S(1)} %get-tuple-element.20, f32[5632]{0:T(1024)S(1)} %get-tuple-element.21, f32[5632]{0:T(1024)S(1)} %get-tuple-element.22, ...), kind=kLoop, calls=%fused_computation.39 | loop fusion | flops 20905984 | bytes 14643200 | tf_op jit(solution)/shard_map/add | solution.py:40
  87.2 47.1 %all-gather.3.cloned.1.call-done = bf16[2816,2240]{1,0:T(8,128)(2,1)} async-done(((bf16[352,2240]{1,0:T(8,128)(2,1)}), bf16[2816,2240]{1,0:T(8,128)(2,1)}) %all-gather.3.cloned.1.call-update) | async-done | bytes 12615696 | tf_op jit(solution)/shard_map/all_gather | solution.py:48
  134.3 10.8 %multiply_convert_fusion = (bf16[1,2,64,2816]{3,2,1,0:T(8,128)(2,1)S(1)}, bf16[1,2,64,2816]{3,2,1,0:T(8,128)(2,1)S(1)}, bf16[1,2,64,2816]{3,2,1,0:T(8,128)(2,1)}) fusion(f32[1,2,64,5632]{3,2,1,0:T(8,128)} %multiply_add_fusion, bf16[2816,2240]{1,0:T(8,128)(2,1)} %all-gather.3.cloned.1.call-done, bf16[1,2,64,2240]{3,2,1,0:T(8,128)(2,1)S(1)} %copy-done), kind=kOutput, calls=%fused_computation.52 | convolution fusion | flops 1620213760 | bytes 18235392 | tf_op jit(solution)/shard_map/dot_general | solution.py:50
  145.1 1.2 fusion.23
  147.0 3.8 %fusion.19 = (f32[5632]{0:T(1024)S(1)}, f32[5632]{0:T(1024)S(1)}, f32[5632]{0:T(1024)S(1)}, f32[5632]{0:T(1024)S(1)}, f32[5632]{0:T(1024)S(1)}, /*index=5*/f32[5...) fusion(bf16[1,1,64,5632]{3,2,1,0:T(8,128)(2,1)S(1)} %copy-done.5, ...), kind=kLoop, calls=%fused_computation.36 | loop fusion | flops 28785152 | bytes 13178880 | tf_op jit(solution)/shard_map/srck,srck->k/dot_general | solution.py:72
  152.0 0.6 stack.34
  152.7 0.6 stack.30
  155.7 0.6 stack.38
  156.4 3.4 %collective-permute-start.2 = (bf16[1,1,64,5632]{3,2,1,0:T(8,128)(2,1)}, bf16[1,1,64,5632]{3,2,1,0:T(8,128)(2,1)S(1)}, u32[]{:S(2)}, u32[]{:S(2)}) collective-permute-start(bf16[1,1,64,5632]{3,2,1,0:T(8,128)(2,1)} %get-tuple-element.37), channel_id=1, source_target_pairs={{0,1},{2,3},{4,5},{6,7},{8,9},{10,11},{12,13},{14,15},{16,17},{18,... | collective-permute-start | bytes 2162696 | tf_op jit(solution)/shard_map/ppermute | solution.py:15
  159.8 1.5 collective-permute-start.3
  161.3 3.2 %stack.39 = f32[9,5632]{1,0:T(8,128)} concatenate(f32[1,5632]{1,0:T(1,128)} %stack.30, f32[1,5632]{1,0:T(1,128)} %stack.31, f32[1,5632]{1,0:T(1,128)} %stack.32, f32[1,5632]{1,0:T(1,128)} %stack.33, f32[1,5632]{1,0:T(1,128)} %stack.34, f32[1,5632]{1,0:T(1,128)} %stack.35, f32[1,5632]{1,0:T(1,128)} %stack.36, f32[1,5632]{1,0:T(1,128)} %stack.37, f32[1,5632]{1,0:T(1,128)} %stack.38), dimensions={0} | concatenate | bytes 405504 | tf_op jit(solution)/shard_map/stack | solution.py:75
  164.5 3.0 %copy.79 = f32[9,5632]{0,1:T(8,128)} copy(f32[9,5632]{1,0:T(8,128)} %stack.39) | data formatting | bytes 405504
  167.5 10.8 %convolution_convert_fusion = bf16[128,2240]{0,1:T(8,128)(2,1)} fusion(bf16[128,2816]{1,0:T(8,128)(2,1)} %bitcast.98, bf16[2816,2240]{1,0:T(8,128)(2,1)} %all-gather.3.cloned.1.call-done), kind=kOutput, calls=%fused_computation.15 | convolution fusion | flops 1615093760 | bytes 13910016 | tf_op jit(solution)/shard_map/dot_general | solution.py:49
  178.3 2.1 copy.15
  180.5 0.8 convert_reduce_fusion
  181.3 27.8 %all-reduce.3 = f32[5632]{0:T(1024)} all-reduce(f32[5632]{0:T(1024)} %convert_reduce_fusion), channel_id=3, replica_groups=mesh['groups'=2,'fsdp'=8,'band'=2] {'fsdp'}, use_global_device_ids=true, to_apply=%region_4.5.clone | all-reduce | flops 5632 | bytes 45056
  209.1 0.8 dynamic-slice.2
  209.9 1.8 copy.80
  211.6 11.1 %all-reduce.4 = (f32[9,704]{1,0:T(8,128)}, f32[704]{0:T(1024)}) all-reduce(f32[9,704]{1,0:T(8,128)} %copy.80, f32[704]{0:T(1024)S(1)} %dynamic-slice.2), channel_id=1, replica_groups=mesh['groups'=2,'fsdp'=8,'band'=2] {'band'}, use_global_device_ids=true, to_apply=%region_0.1 | all-reduce | flops 7040 | bytes 56320 | tf_op jit(solution)/shard_map/psum | solution.py:77
  222.7 1.8 select_maximum_fusion
  224.6 4.5 %fusion.12 = bf16[1,2,64,5632]{3,2,1,0:T(8,128)(2,1)} fusion(bf16[1,4,66,5632]{3,2,1,0:T(8,128)(2,1)S(1)} %select_maximum_fusion, bf16[1,1,64,5632]{3,2,1,0:T(8,128)(2,1)S(1)} %collective-permute-done.2, bf16[1,2,64,2816]{3,2,1,0:T(8,128)(2,1)S(1)} %get-tuple-element.28, bf16[1,2,64,2816]{3,2,1,0:T(8,128)(2,1)S(1)} %get-tuple-element.29, ...), kind=kLoop, calls=%fused_computation.29 | loop fusion | flops 28835840 | bytes 13178880 | tf_op jit(solution)/shard_map/convert_element_type | solution.py:74
  (65 shorter events, 6.0 us)
Async XLA Ops:
  7.2 127.2 %copy-start = (bf16[1,2,64,2240]{3,2,1,0:T(8,128)(2,1)S(1)}, bf16[1,2,64,2240]{3,2,1,0:T(8,128)(2,1)}, u32[]{:S(2)}) copy-start(bf16[1,2,64,2240]{3,2,1,0:T(8,128)(2,1)} %param.9) | copy-start | bytes 1720324
  7.2 9.6 %copy-start.22 = (u32[32]{0:T(128)S(1)}, u32[32]{0:T(128)}, u32[]{:S(2)}) copy-start(u32[32]{0:T(128)} %constant.15) | copy-start | bytes 388
  7.2 73.3 %copy-start.3 = (bf16[1,2,64,5632]{3,2,1,0:T(8,128)(2,1)S(1)}, bf16[1,2,64,5632]{3,2,1,0:T(8,128)(2,1)}, u32[]{:S(2)}) copy-start(bf16[1,2,64,5632]{3,2,1,0:T(8,128)(2,1)} %param.5) | copy-start | bytes 4325380
  7.2 10.9 %copy-start.23 = (bf16[704]{0:T(1024)(128)(2,1)S(1)}, bf16[704]{0:T(1024)(128)(2,1)}, u32[]{:S(2)}) copy-start(bf16[704]{0:T(1024)(128)(2,1)} %param.7) | copy-start | bytes 4228
  7.2 42.4 %copy-start.21 = (bf16[9,704]{1,0:T(8,128)(2,1)S(1)}, bf16[9,704]{1,0:T(8,128)(2,1)}, u32[]{:S(2)}) copy-start(bf16[9,704]{1,0:T(8,128)(2,1)} %param.6) | copy-start | bytes 38020
  7.2 127.1 %all-gather.3.cloned.1.call-start = ((), (), s32[]{:S(2)}) async-start(), calls=%async_computation.1 | async-start | bytes 14598144 | tf_op jit(solution)/shard_map/all_gather | solution.py:48
  8.0 201.9 %reduce-scatter.4.cloned.1.call-start = ((), (), s32[]{:S(2)}) async-start(), calls=%async_computation.2 | async-start | bytes 3244032
  10.6 69.9 %collective-permute-start.1 = (bf16[1,1,64,5632]{3,2,1,0:T(8,128)(2,1)}, bf16[1,1,64,5632]{3,2,1,0:T(8,128)(2,1)S(1)}, u32[]{:S(2)}, u32[]{:S(2)}) collective-permute-start(bf16[1,1,64,5632]{3,2,1,0:T(8,128)(2,1)} %get-tuple-element.39), channel_id=1, source_target_pairs={{1,0},{3,2},{5,4},{7,6},{9,8},{11,10},{13,12},{15,14},{17,16},{19,... | collective-permute-start | bytes 2162696 | tf_op jit(solution)/shard_map/ppermute | solution.py:17
  11.9 68.6 %collective-permute-start = (bf16[1,1,64,5632]{3,2,1,0:T(8,128)(2,1)}, bf16[1,1,64,5632]{3,2,1,0:T(8,128)(2,1)S(1)}, u32[]{:S(2)}, u32[]{:S(2)}) collective-permute-start(bf16[1,1,64,5632]{3,2,1,0:T(8,128)(2,1)} %get-tuple-element.40), channel_id=1, source_target_pairs={{0,1},{2,3},{4,5},{6,7},{8,9},{10,11},{12,13},{14,15},{16,17},{18,... | collective-permute-start | bytes 2162696 | tf_op jit(solution)/shard_map/ppermute | solution.py:15
  80.4 1.2 copy-start.8
  80.4 1.2 copy-start.10
  80.4 1.2 copy-start.12
  80.4 1.2 copy-start.14
  80.4 1.2 copy-start.16
  80.4 1.2 copy-start.18
  80.4 2.8 %copy-start.20 = (f32[5632]{0:T(1024)S(1)}, f32[5632]{0:T(1024)}, u32[]{:S(2)}) copy-start(f32[5632]{0:T(1024)} %convert_element_type.109) | copy-start | bytes 67588
  80.5 1.2 copy-start.4
  80.5 1.2 copy-start.6
  81.6 1.7 copy-start.1
  134.3 12.0 %copy-start.2 = (bf16[1,4,66,5632]{3,2,1,0:T(8,128)(2,1)S(1)}, bf16[1,4,66,5632]{3,2,1,0:T(8,128)(2,1)}, u32[]{:S(2)}) copy-start(bf16[1,4,66,5632]{3,2,1,0:T(8,128)(2,1)} %copy-done.1) | copy-start | bytes 8921092
  145.1 1.4 copy-start.5
  145.1 1.8 copy-start.7
  156.4 66.4 %collective-permute-start.2 = (bf16[1,1,64,5632]{3,2,1,0:T(8,128)(2,1)}, bf16[1,1,64,5632]{3,2,1,0:T(8,128)(2,1)S(1)}, u32[]{:S(2)}, u32[]{:S(2)}) collective-permute-start(bf16[1,1,64,5632]{3,2,1,0:T(8,128)(2,1)} %get-tuple-element.37), channel_id=1, source_target_pairs={{0,1},{2,3},{4,5},{6,7},{8,9},{10,11},{12,13},{14,15},{16,17},{18,... | collective-permute-start | bytes 2162696 | tf_op jit(solution)/shard_map/ppermute | solution.py:15
  159.8 62.9 %collective-permute-start.3 = (bf16[1,1,64,5632]{3,2,1,0:T(8,128)(2,1)}, bf16[1,1,64,5632]{3,2,1,0:T(8,128)(2,1)S(1)}, u32[]{:S(2)}, u32[]{:S(2)}) collective-permute-start(bf16[1,1,64,5632]{3,2,1,0:T(8,128)(2,1)} %get-tuple-element.38), channel_id=1, source_target_pairs={{1,0},{3,2},{5,4},{7,6},{9,8},{11,10},{13,12},{15,14},{17,16},{19,... | collective-permute-start | bytes 2162696 | tf_op jit(solution)/shard_map/ppermute | solution.py:17
  222.7 1.8 copy-start.9
  222.7 1.8 copy-start.11
  222.7 1.8 copy-start.13
  222.7 1.8 copy-start.15
  222.7 1.8 copy-start.17
  222.7 1.8 copy-start.19
Sparse Core Ops, SparseCore 0:
  9.7 124.5 all-gather.2
  167.6 38.5 reduce-scatter.3
where the time goes:
time: 237 us; the launch traced here: 236 us
  blocking collectives  94.7 us (40%)
  waiting for transfers between devices  47.9 us (20%)
  local copies, waits for them, and re-layouts  26.3 us (11%)
  matrix products  21.6 us (9%)
  other arithmetic  18.4 us (8%)
  between operations  15.7 us (7%)
  starting transfers between devices  11.2 us (5%)
    unnamed x2, blocking collectives  58.5 us
    all_gather x1, waiting for transfers between devices, body(): piece = lax.all_gather(w_out, 'fsdp', axis=0, tiled=True)  47.1 us
    all_gather x1, blocking collectives, body(): lax.all_gather(tap_weights, 'fsdp', axis=1, tiled=True)  25.2 us
    psum x1, blocking collectives, body(): tap_grad, bias_grad = lax.psum((tap_grad, bias_grad), 'band')  11.1 us
    dot_general x1, matrix products, body(): out_sum = jnp.dot(glu_flat, piece, preferred_element_type=jnp.float32)  10.8 us
    dot_general x1, matrix products, body(): lax.dot_general(grad_flat, piece, (((1,), (1,)), ((), ())), preferred_ele...  10.8 us
    another operation x10, local copies, waits for them, and re-layouts, body(): tap_grad = jnp.stack(tap_terms)  8.77 us
    unnamed x54, local copies, waits for them, and re-layouts  8.64 us
  transfers between devices with their start and end apart: 6, of which 1 were waited for; matrix products, arithmetic and copies ran while one was open for 15% of the time, Pallas kernels for 0%

commit v1 on v0

--- a/solution.py
+++ b/solution.py
@@ -1,7 +1,17 @@
+import functools
+
 import jax
 import jax.numpy as jnp
 from jax import lax
+from jax.experimental import pallas as pl
+from jax.experimental.pallas import tpu as pltpu
 from jax.sharding import PartitionSpec as P
+
+MESH = pl.DeviceIdType.MESH
+LANES = 128
+PIECE = 32
+F32 = jnp.float32
+BF16 = jnp.bfloat16
 
 
 def with_halo(cells, sides, width):
@@ -21,7 +31,7 @@
     return cells
 
 
-def body(hidden_in, tap_weights, tap_bias, w_out, cotangent):
+def general_body(hidden_in, tap_weights, tap_bias, w_out, cotangent):
     kernel_all, offset_all = (
         lax.all_gather(tap_weights, "fsdp", axis=1, tiled=True),
         lax.all_gather(tap_bias, "fsdp", axis=0, tiled=True),
@@ -47,10 +57,9 @@
     features = grad_flat.shape[1]
     piece = lax.all_gather(w_out, "fsdp", axis=0, tiled=True)
     out_sum = jnp.dot(glu_flat, piece, preferred_element_type=jnp.float32)
-    d_piece = lax.dot_general(
+    d_glu = lax.dot_general(
         grad_flat, piece, (((1,), (1,)), ((), ())), preferred_element_type=jnp.float32
     )
-    out_sum, d_glu = (out_sum, d_piece)
     block_out = out_sum.astype(jnp.bfloat16).reshape(image_count, row_count, col_count, features)
     d_glu = d_glu.reshape(image_count, row_count, col_count, hidden_units)
     slope = sigmoid_gate * (1.0 + gate_half * (1.0 - sigmoid_gate))
@@ -82,6 +91,595 @@
     return (block_out, d_hidden, tap_share, bias_share)
 
 
+def halo_groups(blocks):
+    first = min(2, blocks)
+    second = min(3, blocks - first)
+    sizes = [n for n in (first, second, blocks - first - second) if n > 0]
+    starts = [sum(sizes[:i]) for i in range(len(sizes))]
+    return list(zip(starts, sizes))
+
+
+def unit_kernel(
+    hid, taps, w, cot,
+    out, dhid, tgrad,
+    W, C, H, HH, T, TF, GLU, D, DH, DHS, G, GS, R, PS, PR,
+    bar_dummy,
+    s_own, s_cot, s_d2d_s, s_d2d_r, s_up, s_dn, s_zr, s_ys, s_yr,
+    s_hl, s_hs, s_hr, s_hxs, s_hxr,
+    s_ts, s_tr, s_ds, s_dr, s_ol, s_os, s_or, s_gs, s_gr, s_ps, s_pr,
+):
+    y = lax.axis_index("groups")
+    f = lax.axis_index("fsdp")
+    x = lax.axis_index("band")
+    z, c = f // 2, f % 2
+    sib = z * 2 + (1 - c)
+    nz = lax.axis_size("fsdp") // 2
+    shard, features = w.shape
+    half = W.shape[0]
+    plane = 2 * shard
+    hidden_units = 2 * half
+    blocks = half // LANES
+    steps = half // (2 * PIECE)
+    own_steps = steps // 2
+    s = jnp.where(c == 0, z, nz - 1 - z)
+    up = jnp.where(c == 0, f + 2, f - 2)
+    down = jnp.where(c == 0, f - 2, f + 2)
+    source = s < 2
+    groups = halo_groups(blocks)
+
+    def ascending(core, zz):
+        pos = jnp.where(core == 0, zz, nz - 1 - zz)
+        return (core == 1) != (pos == 0)
+
+    asc = ascending(c, z)
+
+    def block_of(j):
+        return jnp.where(asc, j, blocks - 1 - j)
+
+    def al(v, m):
+        return pl.multiple_of(v, m)
+
+    barrier = pltpu.get_barrier_semaphore()
+    count = 0
+    for df in range(2 * nz):
+        for dx in range(2):
+            if df == 0 and dx == 0:
+                continue
+            pl.semaphore_signal(
+                barrier, inc=1, device_id=(y, lax.rem(f + df, 2 * nz), lax.rem(x + dx, 2)),
+                device_id_type=MESH,
+            )
+            count += 1
+    pl.semaphore_signal(barrier, inc=1, device_id=(1 - y, f, x), device_id_type=MESH)
+    pl.semaphore_wait(barrier, count + 1)
+
+    my_base = (z % 2) * plane
+
+    def own_copy():
+        return pltpu.make_async_copy(w, W.at[pl.ds(al(my_base + c * shard, 16), shard)], s_own)
+
+    def d2d(k):
+        at = jnp.where(c == 1, shard - PIECE * (k + 1), PIECE * k)
+        at = al(at, PIECE)
+        return pltpu.make_async_remote_copy(
+            w.at[pl.ds(at, PIECE)],
+            W.at[pl.ds(al(my_base + c * shard + at, PIECE), PIECE)],
+            s_d2d_s.at[k], s_d2d_r.at[k], device_id=(y, sib, x), device_id_type=MESH,
+        )
+
+    def rows_of(u, yy):
+        return al(jnp.where(c == 0, half - 2 * PIECE * (u + 1), 2 * PIECE * u) + PIECE * yy, PIECE)
+
+    def z_up(u):
+        r = W.at[pl.ds(rows_of(u, y), PIECE)]
+        return pltpu.make_async_remote_copy(
+            r, r, s_up.at[u], s_zr.at[u], device_id=(y, up, x), device_id_type=MESH
+        )
+
+    def z_down(u):
+        r = W.at[pl.ds(rows_of(u, y), PIECE)]
+        return pltpu.make_async_remote_copy(
+            r, r, s_dn.at[u], s_zr.at[u], device_id=(y, down, x), device_id_type=MESH
+        )
+
+    def y_copy(u, yy):
+        r = W.at[pl.ds(rows_of(u, yy), PIECE)]
+        return pltpu.make_async_remote_copy(
+            r, r, s_ys.at[u], s_yr.at[u], device_id=(1 - y, f, x), device_id_type=MESH
+        )
+
+    def lane_at(a, g):
+        st, n = groups[g]
+        return jnp.where(a, LANES * st, LANES * (blocks - st - n))
+
+    def hid_local(g, k):
+        n = groups[g][1] * LANES
+        at = lane_at(asc, g)
+        return pltpu.make_async_copy(
+            hid.at[0, :, :, pl.ds(al(k * hidden_units + c * half + at, LANES), n)],
+            H.at[k, c, :, :, pl.ds(al(at, LANES), n)], s_hl.at[g, k],
+        )
+
+    def hid_sib(g, k, sending):
+        n = groups[g][1] * LANES
+        core = 1 - c if sending else c
+        at = lane_at(ascending(core, z), g)
+        return pltpu.make_async_remote_copy(
+            hid.at[0, :, :, pl.ds(al(k * hidden_units + core * half + at, LANES), n)],
+            H.at[k, c if sending else 1 - c, :, :, pl.ds(al(at, LANES), n)],
+            s_hs.at[g, k], s_hr.at[g, k], device_id=(y, sib, x), device_id_type=MESH,
+        )
+
+    def hid_x_send(core, g, k):
+        n = groups[g][1] * LANES
+        at = lane_at(ascending(core, z), g)
+        return pltpu.make_async_remote_copy(
+            hid.at[0, 1 - x, :, pl.ds(al(k * hidden_units + core * half + at, LANES), n)],
+            HH.at[k, c, :, pl.ds(al(at, LANES), n)],
+            s_hxs.at[core, g, k], s_hxr.at[c, g, k],
+            device_id=(y, 2 * z + core, 1 - x), device_id_type=MESH,
+        )
+
+    def hid_x_recv(img, g, k):
+        n = groups[g][1] * LANES
+        r = HH.at[k, img, :, pl.ds(al(lane_at(asc, g), LANES), n)]
+        return pltpu.make_async_remote_copy(
+            r, r, s_hxs.at[0, g, k], s_hxr.at[img, g, k],
+            device_id=(y, f, 1 - x), device_id_type=MESH,
+        )
+
+    cot_local = pltpu.make_async_copy(cot, C.at[c], s_cot.at[0])
+
+    def cot_sib(img):
+        return pltpu.make_async_remote_copy(
+            cot, C.at[img], s_cot.at[1], s_cot.at[2], device_id=(y, sib, x), device_id_type=MESH
+        )
+
+    tap_core = z % 2
+    tap_slot = 2 * (z // 2) + c
+
+    def tap_send(zz):
+        return pltpu.make_async_remote_copy(
+            taps, T.at[tap_slot], s_ts.at[zz], s_tr.at[tap_slot],
+            device_id=(y, 2 * zz + tap_core, x), device_id_type=MESH,
+        )
+
+    def tap_local(slot):
+        return pltpu.make_async_copy(taps, T.at[slot], s_tr.at[slot])
+
+    def d_halo(b, row):
+        return pltpu.make_async_remote_copy(
+            D.at[b, row], DH.at[b], s_ds.at[b], s_dr.at[b],
+            device_id=(y, f, 1 - x), device_id_type=MESH,
+        )
+
+    is_self = tap_core == c
+    for zz in range(4):
+        @pl.when(jnp.logical_or(jnp.logical_not(is_self), z != zz))
+        def _():
+            tap_send(zz).start()
+
+    @pl.when(is_self)
+    def _():
+        tap_local(tap_slot).start()
+
+    @pl.when(jnp.logical_not(source))
+    def _():
+        for k in range(shard // PIECE):
+            d2d(k).start()
+
+    @pl.when(source)
+    def _():
+        own_copy().start()
+
+    for g in range(len(groups)):
+        for k in range(2):
+            for core in range(2):
+                hid_x_send(core, g, k).start()
+            hid_local(g, k).start()
+            hid_sib(g, k, True).start()
+        if g == 0:
+            cot_local.start()
+            cot_sib(c).start()
+
+    split = (shard // PIECE + 1) // 2
+    n_d2d = shard // PIECE
+
+    @pl.when(source)
+    def _():
+        own_copy().wait()
+
+        @pl.when(s == 1)
+        def _():
+            for u in range(own_steps - 1, split - 1, -1):
+                z_down(u).start()
+
+        first = jnp.where(s == 1, 0, own_steps)
+        for i in range(own_steps):
+            for m in (2 * i, 2 * i + 1):
+                if m < n_d2d:
+                    at = al(jnp.where(c == 0, plane - PIECE * (m + 1), PIECE * m), PIECE)
+                    r = W.at[pl.ds(al(my_base + at, PIECE), PIECE)]
+                    pltpu.make_async_remote_copy(
+                        r, r, s_d2d_s.at[m], s_d2d_r.at[m],
+                        device_id=(y, sib, x), device_id_type=MESH,
+                    ).wait_recv()
+            z_up(first + i).start()
+
+        @pl.when(s == 1)
+        def _():
+            for u in range(split - 1, -1, -1):
+                z_down(u).start()
+
+    for slot in range(4):
+        tap_local(slot).wait()
+    for k in range(2):
+        TF[k] = jnp.concatenate(
+            [T[2 * k].astype(F32), T[2 * k + 1].astype(F32)], axis=1
+        )
+    cot_local.wait()
+    cot_sib(1 - c).wait_recv()
+
+    col = lax.broadcasted_iota(jnp.int32, (H.shape[3], LANES), 0)
+    cols = H.shape[3]
+
+    def before(a):
+        return jnp.where(col == 0, 0.0, pltpu.roll(a, 1, 0))
+
+    def after(a):
+        return jnp.where(col == cols - 1, 0.0, pltpu.roll(a, cols - 1, 0))
+
+    def needed(u):
+        return jnp.logical_or(
+            s >= 2,
+            jnp.logical_or(
+                jnp.logical_and(s == 0, u < own_steps), jnp.logical_and(s == 1, u >= own_steps)
+            ),
+        )
+
+    def u_of(i):
+        return jnp.where(s == 0, steps - 1 - i, i)
+
+    def take(j):
+        for h in range(2):
+            u = u_of(2 * j + h)
+
+            @pl.when(needed(u))
+            def _():
+                z_up(u).wait_recv()
+
+                @pl.when(jnp.logical_or(s == 1, s == 2))
+                def _():
+                    z_up(u).start()
+
+                y_copy(u, y).start()
+
+    def halo_in(g):
+        for k in range(2):
+            hid_local(g, k).wait()
+            hid_sib(g, k, False).wait_recv()
+            for img in range(2):
+                hid_x_recv(img, g, k).wait_recv()
+
+    def stage_a(j):
+        b = block_of(j)
+        lane = pl.ds(al(b * LANES, LANES), LANES)
+        for h in range(2):
+            u = u_of(2 * j + h)
+
+            @pl.when(needed(u))
+            def _():
+                y_copy(u, 1 - y).wait_recv()
+
+        wb = W[lane, :]
+        ext = {}
+        tf = [TF[k, :, lane] for k in range(2)]
+        sums = [[None] * 10, [None] * 10]
+        for img in range(2):
+            dg = lax.dot_general(
+                C[img], wb, (((1,), (1,)), ((), ())), preferred_element_type=F32
+            )
+            pre = [[], []]
+            rows = [None, None]
+            for k in range(2):
+                hal = HH[k, img, :, lane].astype(F32)
+                rows[k] = [
+                    jnp.where(x == 1, hal, 0.0),
+                    H[k, img, 0, :, lane].astype(F32),
+                    H[k, img, 1, :, lane].astype(F32),
+                    jnp.where(x == 0, hal, 0.0),
+                ]
+                for r in range(2):
+                    a = [
+                        sum(tf[k][3 * i + jj : 3 * i + jj + 1] * rows[k][r + i] for i in range(3))
+                        for jj in range(3)
+                    ]
+                    pre[k].append(before(a[0]) + (a[1] + tf[k][9:10]) + after(a[2]))
+            for r in range(2):
+                v, gt = pre[0][r], pre[1][r]
+                sg = jax.nn.sigmoid(gt)
+                si = gt * sg
+                at = img * 2 * cols + r * cols
+                GLU[at : at + cols, lane] = (v * si).astype(BF16)
+                d = dg[r * cols : (r + 1) * cols]
+                dv = (d * si).astype(BF16)
+                dq = (d * v * (sg * (1.0 + gt * (1.0 - sg)))).astype(BF16)
+                D[b, r, 0, img] = dv
+                D[b, r, 1, img] = dq
+                for k, dd in ((0, dv), (1, dq)):
+                    dd = dd.astype(F32)
+                    shifted = (after(dd), dd, before(dd))
+                    for i in range(3):
+                        for jj in range(3):
+                            t = rows[k][r + i] * shifted[jj]
+                            n = 3 * i + jj
+                            sums[k][n] = t if sums[k][n] is None else sums[k][n] + t
+                    sums[k][9] = dd if sums[k][9] is None else sums[k][9] + dd
+        d_halo(b, 1 - x).start()
+        for k in range(2):
+            for n in range(10):
+                G[k, n : n + 1, lane] = jnp.sum(sums[k][n], axis=0, keepdims=True)
+
+    def out_lanes(b, k):
+        return pl.ds(al(k * hidden_units + c * half + b * LANES, LANES), LANES)
+
+    def o_local(b, k):
+        lane = pl.ds(al(b * LANES, LANES), LANES)
+        return pltpu.make_async_copy(
+            DHS.at[k, c, :, :, lane], dhid.at[0, :, :, out_lanes(b, k)], s_ol.at[b, k]
+        )
+
+    def o_sib(b, k):
+        lane = pl.ds(al(b * LANES, LANES), LANES)
+        return pltpu.make_async_remote_copy(
+            DHS.at[k, 1 - c, :, :, lane], dhid.at[0, :, :, out_lanes(b, k)],
+            s_os.at[b, k], s_or.at[b, k], device_id=(y, sib, x), device_id_type=MESH,
+        )
+
+    def o_sib_in(b, k):
+        lane = pl.ds(al(b * LANES, LANES), LANES)
+        return pltpu.make_async_remote_copy(
+            DHS.at[k, c, :, :, lane],
+            dhid.at[0, :, :, pl.ds(al(k * hidden_units + (1 - c) * half + b * LANES, LANES), LANES)],
+            s_os.at[b, k], s_or.at[b, k], device_id=(y, sib, x), device_id_type=MESH,
+        )
+
+    def stage_b(j):
+        b = block_of(j)
+        lane = pl.ds(al(b * LANES, LANES), LANES)
+        d_halo(b, 1 - x).wait_recv()
+        for k in range(2):
+            tf = TF[k, :, lane]
+            for img in range(2):
+                hal = DH[b, k, img].astype(F32)
+                rows = [
+                    jnp.where(x == 1, hal, 0.0),
+                    D[b, 0, k, img].astype(F32),
+                    D[b, 1, k, img].astype(F32),
+                    jnp.where(x == 0, hal, 0.0),
+                ]
+                for r in range(2):
+                    a = [
+                        sum(tf[3 * i + jj : 3 * i + jj + 1] * rows[r + 2 - i] for i in range(3))
+                        for jj in range(3)
+                    ]
+                    DHS[k, img, r, :, lane] = (after(a[0]) + a[1] + before(a[2])).astype(BF16)
+            o_local(b, k).start()
+            o_sib(b, k).start()
+
+    take(0)
+
+    @pl.loop(0, blocks)
+    def _(j):
+        for g in range(len(groups)):
+            @pl.when(j == groups[g][0])
+            def _():
+                halo_in(g)
+
+        @pl.when(j < blocks - 1)
+        def _():
+            take(j + 1)
+
+        stage_a(j)
+
+        @pl.when(j >= 2)
+        def _():
+            stage_b(j - 2)
+
+    for k in range(2):
+        GS[2 * k] = G[k, :, 0:plane]
+        GS[2 * k + 1] = G[k, :, plane:]
+
+    my_slot = 2 * z + x
+
+    def g_dev(n, xx):
+        return 2 * (2 * (n // 2) + c) + (n % 2)
+
+    def g_send(n, xx):
+        return pltpu.make_async_remote_copy(
+            GS.at[n], R.at[my_slot], s_gs.at[n, xx], s_gr.at[my_slot],
+            device_id=(y, g_dev(n, xx), xx), device_id_type=MESH,
+        )
+
+    def g_self(n, xx):
+        return jnp.logical_and(g_dev(n, xx) == f, x == xx)
+
+    for n in range(4):
+        for xx in range(2):
+            @pl.when(g_self(n, xx))
+            def _():
+                pltpu.make_async_copy(GS.at[n], R.at[my_slot], s_gr.at[my_slot]).start()
+
+            @pl.when(jnp.logical_not(g_self(n, xx)))
+            def _():
+                g_send(n, xx).start()
+
+    tokens = 2 * cols
+    part = []
+    n_at = 0
+    while n_at < features:
+        part.append((n_at, min(512, features - n_at)))
+        n_at += 512
+
+    def product(img, at, n):
+        g = GLU[pl.ds(al(img * tokens, tokens), tokens), :]
+        return jnp.dot(g, W[:, at : at + n], preferred_element_type=F32)
+
+    for at, n in part:
+        PS[:, at : at + n] = product(1 - c, at, n).astype(BF16)
+    p_copy = pltpu.make_async_remote_copy(
+        PS, PR, s_ps, s_pr, device_id=(y, sib, x), device_id_type=MESH
+    )
+    p_copy.start()
+    stage_b(blocks - 2)
+    stage_b(blocks - 1)
+    mine = [product(c, at, n) for at, n in part]
+    p_copy.wait_recv()
+    for (at, n), m in zip(part, mine):
+        out[:, at : at + n] = (m + PR[:, at : at + n].astype(F32)).astype(BF16)
+
+    for slot in range(8):
+        pltpu.make_async_copy(GS.at[0], R.at[slot], s_gr.at[slot]).wait()
+    total = R[0]
+    for slot in range(1, 8):
+        total = total + R[slot]
+    tgrad[...] = total
+
+    for n in range(4):
+        for xx in range(2):
+            @pl.when(jnp.logical_not(g_self(n, xx)))
+            def _():
+                g_send(n, xx).wait_send()
+    p_copy.wait_send()
+    for zz in range(4):
+        @pl.when(jnp.logical_or(jnp.logical_not(is_self), z != zz))
+        def _():
+            tap_send(zz).wait_send()
+
+    @pl.when(jnp.logical_not(source))
+    def _():
+        for k in range(n_d2d):
+            d2d(k).wait_send()
+
+    cot_sib(c).wait_send()
+    for g in range(len(groups)):
+        for k in range(2):
+            for core in range(2):
+                hid_x_send(core, g, k).wait_send()
+            hid_sib(g, k, True).wait_send()
+
+    @pl.loop(0, steps)
+    def _(u):
+        @pl.when(jnp.logical_or(s == 1, jnp.logical_or(s == 2, jnp.logical_and(s == 0, u >= own_steps))))
+        def _():
+            z_up(u).wait_send()
+
+        @pl.when(jnp.logical_and(s == 1, u < own_steps))
+        def _():
+            z_down(u).wait_send()
+
+        @pl.when(needed(u))
+        def _():
+            y_copy(u, y).wait_send()
+
+    @pl.loop(0, blocks)
+    def _(b):
+        d_halo(b, 1 - x).wait_send()
+        for k in range(2):
+            o_local(b, k).wait()
+            o_sib(b, k).wait_send()
+            o_sib_in(b, k).wait_recv()
+
+
+def fused_body(hidden_in, tap_weights, tap_bias, w_out, cotangent):
+    _, rows, cols, channels = hidden_in.shape
+    shard, features = w_out.shape
+    own_channels = tap_weights.shape[1]
+    half = channels // 4
+    blocks = half // LANES
+    tokens = rows * cols
+    taps = jnp.concatenate(
+        [tap_weights, tap_bias[None], jnp.zeros((6, own_channels), BF16)], axis=0
+    )
+    steps = half // (2 * PIECE)
+    n_groups = len(halo_groups(blocks))
+    dma = pltpu.SemaphoreType.DMA
+    flops = 2 * 2 * 2 * tokens * half * features
+    out, d_hidden, tgrad = pl.pallas_call(
+        unit_kernel,
+        out_shape=(
+            jax.ShapeDtypeStruct((tokens, features), BF16),
+            jax.ShapeDtypeStruct(hidden_in.shape, BF16),
+            jax.ShapeDtypeStruct((16, own_channels), F32),
+        ),
+        in_specs=[
+            pl.BlockSpec(memory_space=pl.ANY),
+            pl.BlockSpec(memory_space=pltpu.VMEM),
+            pl.BlockSpec(memory_space=pl.ANY),
+            pl.BlockSpec(memory_space=pl.ANY),
+        ],
+        out_specs=(
+            pl.BlockSpec(memory_space=pltpu.VMEM),
+            pl.BlockSpec(memory_space=pl.ANY),
+            pl.BlockSpec(memory_space=pltpu.VMEM),
+        ),
+        scratch_shapes=[
+            pltpu.VMEM((half, features), BF16),
+            pltpu.VMEM((2, tokens, features), BF16),
+            pltpu.VMEM((2, 2, rows, cols, half), BF16),
+            pltpu.VMEM((2, 2, cols, half), BF16),
+            pltpu.VMEM((4, 16, own_channels), BF16),
+            pltpu.VMEM((2, 16, half), F32),
+            pltpu.VMEM((2 * tokens, half), BF16),
+            pltpu.VMEM((blocks, rows, 2, 2, cols, LANES), BF16),
+            pltpu.VMEM((blocks, 2, 2, cols, LANES), BF16),
+            pltpu.VMEM((2, 2, rows, cols, half), BF16),
+            pltpu.VMEM((2, 16, half), F32),
+            pltpu.VMEM((4, 16, own_channels), F32),
+            pltpu.VMEM((8, 16, own_channels), F32),
+            pltpu.VMEM((tokens, features), BF16),
+            pltpu.VMEM((tokens, features), BF16),
+            pltpu.SemaphoreType.REGULAR,
+            dma, dma((3,)), dma((shard // PIECE,)), dma((shard // PIECE,)),
+            dma((steps,)), dma((steps // 2,)), dma((steps,)), dma((steps,)), dma((steps,)),
+            dma((n_groups, 2)), dma((n_groups, 2)), dma((n_groups, 2)),
+            dma((2, n_groups, 2)), dma((2, n_groups, 2)),
+            dma((4,)), dma((4,)), dma((blocks,)), dma((blocks,)),
+            dma((blocks, 2)), dma((blocks, 2)), dma((blocks, 2)),
+            dma((4, 2)), dma((8,)), dma, dma,
+        ],
+        compiler_params=pltpu.CompilerParams(
+            collective_id=0, has_side_effects=True, vmem_limit_bytes=56 * 1024 * 1024
+        ),
+        cost_estimate=pl.CostEstimate(flops=flops, bytes_accessed=8 << 20, transcendentals=0),
+    )(hidden_in, taps, w_out, cotangent.reshape(tokens, features))
+    return (
+        out.reshape(cotangent.shape), d_hidden, tgrad[:9], tgrad[9],
+    )
+
+
+def fits(mesh, hidden_in, tap_weights, tap_bias, w_out, cotangent):
+    if (mesh.shape["groups"], mesh.shape["fsdp"], mesh.shape["band"]) != (2, 8, 2):
+        return False
+    images, rows, cols, channels = hidden_in.shape
+    return (
+        images == 1
+        and rows == 2
+        and cols % 16 == 0
+        and (channels // 4) % (2 * LANES) == LANES
+        and w_out.shape[0] % PIECE == 0
+        and (w_out.shape[0] // PIECE) % 2 == 1
+        and 4 * w_out.shape[0] == channels // 4
+        and 8 * tap_weights.shape[1] == channels
+    )
+
+
+def body(mesh, *args):
+    if fits(mesh, *args):
+        return fused_body(*args)
+    return general_body(*args)
+
+
 def solution(mesh):
     placed = (
         P(("groups", "fsdp"), "band", None, None),
@@ -91,7 +689,7 @@
         P(("groups", "fsdp"), "band", None, None),
     )
     return jax.shard_map(
-        body,
+        functools.partial(body, mesh),
         mesh=mesh,
         in_specs=placed,
         out_specs=(

time: 237 us -> 97 us (0.41)
  blocking collectives: 94.7 us -> 0 us
  Pallas kernels: 0 us -> 86.8 us
  waiting for transfers between devices: 47.9 us -> 0 us
  matrix products: 21.6 us -> 0 us
  local copies, waits for them, and re-layouts: 26.3 us -> 7.21 us
  other arithmetic: 18.4 us -> 1.42 us
  between operations: 15.7 us -> 0.64 us
  starting transfers between devices: 11.2 us -> 0 us
    pallas_call x0 -> x1, Pallas kernels: none -> 86.8 us  [fused_body(): pl.pallas_call(unit_kernel, out_shape=(jax.ShapeDtypeStruct((tokens, feat...]
    unnamed x2 -> x0, blocking collectives: 58.5 us -> none
    all_gather x1 -> x0, waiting for transfers between devices: 47.1 us -> none  [body(): piece = lax.all_gather(w_out, 'fsdp', axis=0, tiled=True)]
    all_gather x1 -> x0, blocking collectives: 25.2 us -> none  [body(): lax.all_gather(tap_weights, 'fsdp', axis=1, tiled=True)]
    dot_general x2 -> x0, matrix products: 21.6 us -> none  [the longest x1 10.8 us: body(): out_sum = jnp.dot(glu_flat, piece, preferred_element_type=jnp.float32)]
    ppermute x4 -> x0, starting transfers between devices: 11.1 us -> none  [the longest x2 8.37 us: with_halo(): lax.ppermute(tail, axis, [(i, (i + 1) % count) for i in range(ends)])]
    psum x1 -> x0, blocking collectives: 11.1 us -> none  [body(): tap_grad, bias_grad = lax.psum((tap_grad, bias_grad), 'band')]
    another operation x10 -> x0, local copies, waits for them, and re-layouts: 8.77 us -> none  [body(): tap_grad = jnp.stack(tap_terms)]
  transfers between devices with their start and end apart: 6 -> 0, of which waited for: 1 -> 0; matrix products, arithmetic and copies ran while one was open for 15% -> 0% of each run, Pallas kernels for 0% -> 0%
where the time goes in v1:
time: 97 us; the launch traced here: 96.1 us
  Pallas kernels  86.8 us (89%)
  local copies, waits for them, and re-layouts  7.21 us (7%)
  other arithmetic  1.42 us (1%)
    pallas_call x1, Pallas kernels, fused_body(): pl.pallas_call(unit_kernel, out_shape=(jax.ShapeDtypeStruct((tokens, feat...  86.8 us
    unnamed x5, local copies, waits for them, and re-layouts  5.1 us

profile of v1, /device:TPU:0, one launch (start us, length us, event | category | flops | bytes accessed | tf_op | source)
XLA Modules:
  0.0 96.1 jit_solution(3901780131122965245)
XLA Ops:
  0.6 0.7 broadcast_in_dim.6
  1.3 0.1 pad.2.clone
  1.4 1.4 %maximum_maximum_fusion.taps = bf16[16,704]{1,0:T(8,128)(2,1)} fusion(bf16[1,704]{1,0:T(2,128)(2,1)S(1)} %broadcast_in_dim.6, bf16[9,704]{1,0:T(8,128)(2,1)} %param.6, bf16[16]{0:T(256)(128)(2,1)S(1)} %pad.2.clone), kind=kLoop, calls=%fused_computation | loop fusion | flops 67584 | bytes 36640 | tf_op jit(solution)/shard_map/concatenate | solution.py:601
  2.8 86.8 %shard_map.84 = (bf16[128,2240]{1,0:T(8,128)(2,1)}, bf16[1,2,64,5632]{3,2,1,0:T(8,128)(2,1)}, f32[16,704]{1,0:T(8,128)}) custom-call(bf16[1,2,64,5632]{3,2,1,0:T(8,128)(2,1)} %hid.1, bf16[16,704]{1,0:T(8,128)(2,1)} %maximum_maximum_fusion.taps, bf16[352,2240]{1,0:T(8,128)(2,1)} %w.1, bf16[128,2240]{1,0:T(8,128)(2,1)} %bitcast.5), custom_call_target="tpu_custom_call" | custom-call | flops 3229614080 | bytes 8388608 | tf_op jit(solution)/shard_map/pallas_call | solution.py:608
  89.7 1.3 %slice_reduce_fusion = f32[704]{0:T(1024)} fusion(f32[16,704]{1,0:T(8,128)} %get-tuple-element.9), kind=kLoop, calls=%fused_computation.1 | loop fusion | bytes 5632 | tf_op jit(solution)/shard_map/slice | solution.py:657
  91.0 1.9 %copy.12 = bf16[1,2,64,2240]{3,2,1,0:T(8,128)(2,1)} copy(bf16[1,2,64,2240]{3,2,1,0:T(8,128)(2,1)} %bitcast.3) | data formatting | bytes 1146880
  92.9 0.0 copy-start
  92.9 2.6 %copy.13 = bf16[1,2,64,5632]{3,2,1,0:T(8,128)(2,1)} copy(bf16[1,2,64,5632]{3,2,1,0:T(8,128)(2,1)} %get-tuple-element.15) | data formatting | bytes 2883584
  95.5 0.0 copy-done
  95.5 0.6 copy.14
  (1 shorter events, 0.0 us)
Async XLA Ops:
  92.9 2.6 %copy-start = (f32[16,704]{1,0:T(8,128)S(1)}, f32[16,704]{1,0:T(8,128)}, u32[]{:S(2)}) copy-start(f32[16,704]{1,0:T(8,128)} %get-tuple-element.9) | copy-start | bytes 135172

commit v2 on v1

--- a/solution.py
+++ b/solution.py
@@ -10,6 +10,7 @@
 MESH = pl.DeviceIdType.MESH
 LANES = 128
 PIECE = 32
+AHEAD = 4
 F32 = jnp.float32
 BF16 = jnp.bfloat16
 
@@ -100,10 +101,10 @@
 
 
 def unit_kernel(
-    hid, taps, w, cot,
-    out, dhid, tgrad,
+    hid, tap_in, bias_in, w, cot,
+    out, dhid, tgrad, bgrad,
     W, C, H, HH, T, TF, GLU, D, DH, DHS, G, GS, R, PS, PR,
-    bar_dummy,
+    taps,
     s_own, s_cot, s_d2d_s, s_d2d_r, s_up, s_dn, s_zr, s_ys, s_yr,
     s_hl, s_hs, s_hr, s_hxs, s_hxr,
     s_ts, s_tr, s_ds, s_dr, s_ol, s_os, s_or, s_gs, s_gr, s_ps, s_pr,
@@ -139,6 +140,10 @@
     def al(v, m):
         return pl.multiple_of(v, m)
 
+    taps[...] = jnp.zeros_like(taps)
+    taps[0:9] = tap_in[...].astype(F32)
+    taps[9:10] = bias_in[...].astype(F32)
+
     barrier = pltpu.get_barrier_semaphore()
     count = 0
     for df in range(2 * nz):
@@ -315,7 +320,7 @@
         tap_local(slot).wait()
     for k in range(2):
         TF[k] = jnp.concatenate(
-            [T[2 * k].astype(F32), T[2 * k + 1].astype(F32)], axis=1
+            [T[2 * k], T[2 * k + 1]], axis=1
         )
     cot_local.wait()
     cot_sib(1 - c).wait_recv()
@@ -467,7 +472,8 @@
             o_local(b, k).start()
             o_sib(b, k).start()
 
-    take(0)
+    for first_j in range(AHEAD):
+        take(first_j)
 
     @pl.loop(0, blocks)
     def _(j):
@@ -476,9 +482,9 @@
             def _():
                 halo_in(g)
 
-        @pl.when(j < blocks - 1)
-        def _():
-            take(j + 1)
+        @pl.when(j < blocks - AHEAD)
+        def _():
+            take(j + AHEAD)
 
         stage_a(j)
 
@@ -543,7 +549,8 @@
     total = R[0]
     for slot in range(1, 8):
         total = total + R[slot]
-    tgrad[...] = total
+    tgrad[...] = total[0:9]
+    bgrad[...] = total[9:10]
 
     for n in range(4):
         for xx in range(2):
@@ -598,22 +605,21 @@
     half = channels // 4
     blocks = half // LANES
     tokens = rows * cols
-    taps = jnp.concatenate(
-        [tap_weights, tap_bias[None], jnp.zeros((6, own_channels), BF16)], axis=0
-    )
     steps = half // (2 * PIECE)
     n_groups = len(halo_groups(blocks))
     dma = pltpu.SemaphoreType.DMA
     flops = 2 * 2 * 2 * tokens * half * features
-    out, d_hidden, tgrad = pl.pallas_call(
+    out, d_hidden, tgrad, bgrad = pl.pallas_call(
         unit_kernel,
         out_shape=(
             jax.ShapeDtypeStruct((tokens, features), BF16),
             jax.ShapeDtypeStruct(hidden_in.shape, BF16),
-            jax.ShapeDtypeStruct((16, own_channels), F32),
+            jax.ShapeDtypeStruct((9, own_channels), F32),
+            jax.ShapeDtypeStruct((1, own_channels), F32),
         ),
         in_specs=[
             pl.BlockSpec(memory_space=pl.ANY),
+            pl.BlockSpec(memory_space=pltpu.VMEM),
             pl.BlockSpec(memory_space=pltpu.VMEM),
             pl.BlockSpec(memory_space=pl.ANY),
             pl.BlockSpec(memory_space=pl.ANY),
@@ -622,13 +628,14 @@
             pl.BlockSpec(memory_space=pltpu.VMEM),
             pl.BlockSpec(memory_space=pl.ANY),
             pl.BlockSpec(memory_space=pltpu.VMEM),
+            pl.BlockSpec(memory_space=pltpu.VMEM),
         ),
         scratch_shapes=[
             pltpu.VMEM((half, features), BF16),
             pltpu.VMEM((2, tokens, features), BF16),
             pltpu.VMEM((2, 2, rows, cols, half), BF16),
             pltpu.VMEM((2, 2, cols, half), BF16),
-            pltpu.VMEM((4, 16, own_channels), BF16),
+            pltpu.VMEM((4, 16, own_channels), F32),
             pltpu.VMEM((2, 16, half), F32),
             pltpu.VMEM((2 * tokens, half), BF16),
             pltpu.VMEM((blocks, rows, 2, 2, cols, LANES), BF16),
@@ -639,7 +646,7 @@
             pltpu.VMEM((8, 16, own_channels), F32),
             pltpu.VMEM((tokens, features), BF16),
             pltpu.VMEM((tokens, features), BF16),
-            pltpu.SemaphoreType.REGULAR,
+            pltpu.VMEM((16, own_channels), F32),
             dma, dma((3,)), dma((shard // PIECE,)), dma((shard // PIECE,)),
             dma((steps,)), dma((steps // 2,)), dma((steps,)), dma((steps,)), dma((steps,)),
             dma((n_groups, 2)), dma((n_groups, 2)), dma((n_groups, 2)),
@@ -652,9 +659,9 @@
             collective_id=0, has_side_effects=True, vmem_limit_bytes=56 * 1024 * 1024
         ),
         cost_estimate=pl.CostEstimate(flops=flops, bytes_accessed=8 << 20, transcendentals=0),
-    )(hidden_in, taps, w_out, cotangent.reshape(tokens, features))
+    )(hidden_in, tap_weights, tap_bias.reshape(1, own_channels), w_out, cotangent.reshape(tokens, features))
     return (
-        out.reshape(cotangent.shape), d_hidden, tgrad[:9], tgrad[9],
+        out.reshape(cotangent.shape), d_hidden, tgrad, bgrad.reshape(own_channels),
     )
 
 

time: 97 us -> 90.2 us (0.930)
  Pallas kernels: 86.8 us -> 81.2 us
    pallas_call x1, Pallas kernels: 86.8 us -> 81.2 us  [fused_body(): pl.pallas_call(unit_kernel, out_shape=(jax.ShapeDtypeStruct((tokens, feat...]
    concatenate x1 -> x0, other arithmetic: 1.42 us -> none  [fused_body(): jnp.concatenate([tap_weights, tap_bias[None], jnp.zeros((6, own_channels)...]
    slice x1 -> x0, local copies, waits for them, and re-layouts: 1.34 us -> none  [fused_body(): return (out.reshape(cotangent.shape), d_hidden, tgrad[:9], tgrad[9])]
    pallas_call x0 -> x1, other arithmetic: none -> 1.28 us  [fused_body(): pl.pallas_call(unit_kernel, out_shape=(jax.ShapeDtypeStruct((tokens, feat...]
    reshape x0 -> x1, local copies, waits for them, and re-layouts: none -> 1.26 us  [fused_body(): tap_bias.reshape(1, own_channels)]
where the time goes in v2:
time: 90.2 us; the launch traced here: 89.5 us
  Pallas kernels  81.2 us (90%)
  local copies, waits for them, and re-layouts  6.36 us (7%)
  other arithmetic  1.28 us (1%)
    pallas_call x1, Pallas kernels, fused_body(): pl.pallas_call(unit_kernel, out_shape=(jax.ShapeDtypeStruct((tokens, feat...  81.2 us
    unnamed x5, local copies, waits for them, and re-layouts  5.1 us

profile of v2, /device:TPU:0, one launch (start us, length us, event | category | flops | bytes accessed | tf_op | source)
XLA Modules:
  0.0 89.5 jit_solution(13933554125243268034)
XLA Ops:
  0.6 1.3 %reshape.20.bias_in = bf16[1,704]{1,0:T(2,128)(2,1)} reshape(bf16[704]{0:T(1024)(128)(2,1)} %param.7) | data formatting | bytes 2816 | tf_op jit(solution)/shard_map/reshape | solution.py:662
  1.9 81.2 %shard_map.84 = (bf16[128,2240]{1,0:T(8,128)(2,1)}, bf16[1,2,64,5632]{3,2,1,0:T(8,128)(2,1)}, f32[9,704]{1,0:T(8,128)}, f32[1,704]{1,0:T(1,128)}) custom-call(bf16[1,2,64,5632]{3,2,1,0:T(8,128)(2,1)} %hid.1, bf16[9,704]{1,0:T(8,128)(2,1)} %tap_in.1, bf16[1,704]{1,0:T(2,128)(2,1)} %reshape.20.bias_in, bf16[352,2240]{1,0:T(8,128)(2,1)} %w.1, ...), custom_call_target="tpu_custom_call" | custom-call | flops 3229614080 | bytes 8388608 | tf_op jit(solution)/shard_map/pallas_call | solution.py:612
  83.1 1.3 %reduce = f32[704]{0:T(1024)} reduce(f32[1,704]{1,0:T(1,128)} %get-tuple-element.11, f32[]{:T(128)} %constant.2), dimensions={0}, to_apply=%get-tuple-element.11.reduce_sub_computation | reduce | bytes 5636 | tf_op jit(solution)/shard_map/pallas_call | solution.py:612
  84.4 1.9 %copy.12 = bf16[1,2,64,2240]{3,2,1,0:T(8,128)(2,1)} copy(bf16[1,2,64,2240]{3,2,1,0:T(8,128)(2,1)} %bitcast.2) | data formatting | bytes 1146880
  86.3 0.0 copy-start
  86.3 2.6 %copy.13 = bf16[1,2,64,5632]{3,2,1,0:T(8,128)(2,1)} copy(bf16[1,2,64,5632]{3,2,1,0:T(8,128)(2,1)} %get-tuple-element.17) | data formatting | bytes 2883584
  88.9 0.0 copy-done
  88.9 0.6 copy.14
Async XLA Ops:
  86.3 2.6 %copy-start = (f32[9,704]{1,0:T(8,128)S(1)}, f32[9,704]{1,0:T(8,128)}, u32[]{:S(2)}) copy-start(f32[9,704]{1,0:T(8,128)} %get-tuple-element.18) | copy-start | bytes 76036
